TPU v7x, 32 devices: a whole 2x2x4 slice. The times are simulated.
32 devices in a mesh: rep: 2 (over y), dp: 16 (over z, x, core).
Axes of the slice: x: 2, y: 2, z: 4, core: 2. Of those that a mesh axis runs over, the one named last changes fastest.
Arguments:
- images: bfloat16 [256, 2, 1280], P(('rep', 'dp')), may hold values from -6 to 6
- weight: bfloat16 [1280, 8192], P(None, 'dp'), may hold values from -0.3354102 to 0.3354102, as said below
Outputs:
- image_grad: float32 [256, 2, 1280], P(('rep', 'dp'))
- weight_grad: float32 [1280, 8192], P(None, 'dp')
Inputs may be any that keep to these rules, and one draw needn't show every extreme that they name: `weight`: a projection whose columns have different scales.
All inputs are finite; a program needn't handle non-finite values.
Results may differ from a plain program's by a relative error of at most 0.0021.
Values may be sent and summed in bfloat16 or wider, within the bound.
No kernel may reach another device: no remote copies, remote signals or barrier semaphores. Data moves between devices by JAX's collectives and lax.ppermute only.
A program may use at most 64 MiB of HBM per device.

v0:
```python
import functools

import jax
import jax.numpy as jnp
from jax import lax
from jax.experimental import pallas as pl
from jax.experimental.pallas import tpu as pltpu
from jax.sharding import PartitionSpec as P

invariance_weight = 25.0
variance_weight = 25.0
covariance_weight = 1.0
loss_scale = 8192.0
epsilon_var = 0.0001

F32 = jnp.float32
BF16 = jnp.bfloat16
VMEM = pl.BlockSpec(memory_space=pltpu.VMEM)
SMEM = pl.BlockSpec(memory_space=pltpu.SMEM)
CORE, ACROSS, QUAD = 1, 2, 4
EXTRA = 8


def swap(block, axis, bits):
    return lax.ppermute(block, axis, [(i, i ^ bits) for i in range(lax.axis_size(axis))])


def slot_of(device, me, outer):
    rel = device ^ me
    low, high = rel % QUAD, rel // QUAD
    return ((low // 2) * outer + high) * 2 + low % 2


def centre(z):
    return z - jnp.mean(z, axis=0, keepdims=True)


def nt_dot(a, b):
    return lax.dot_general(a, b, (((1,), (1,)), ((), ())), preferred_element_type=F32)


def half_masks(half, count):
    row = lax.broadcasted_iota(jnp.int32, (half, count), 0)
    lane = lax.broadcasted_iota(jnp.int32, (half, count), 1)
    return (lane < half) & (row < lane), row == lane, lane < half


def whole(near_ref, far_ref):
    return jnp.concatenate([near_ref[...], far_ref[...]], axis=0)


def split_kernel(me_ref, *refs):
    second = me_ref[0] % 2 == 1
    *image_refs, rows_ref = refs
    own = image_refs[0].shape[0]
    parts = [jnp.where(second, ref[:, 1, :], ref[:, 0, :]) for ref in image_refs]
    rows_ref[...] = jnp.concatenate(parts, axis=0)


def gram_kernel(own, me_ref, near_ref, far_ref, c_ref, packed_ref, sorted_ref):
    me = me_ref[0]
    count, width = c_ref.shape
    devices = count // own
    outer = devices // QUAD
    half = count // 2
    centred = centre(whole(near_ref, far_ref)).reshape(devices, own, width)
    for slot in range(devices):
        rel = (slot // 2 % outer) * QUAD + (slot // 2 // outer) * 2 + slot % 2
        sorted_ref[rel ^ me] = centred[slot]
    c = sorted_ref[...].reshape(count, width).astype(BF16)
    c_ref[...] = c
    gram = nt_dot(c, c)
    upper, diagonal, _ = half_masks(half, count)
    turned = pltpu.roll(gram[half:], half, 1)
    packed_ref[:half] = jnp.where(upper, turned, gram[:half])
    second = jnp.sum(jnp.where(diagonal, turned, 0.0), axis=0, keepdims=True)
    packed_ref[half:] = jnp.broadcast_to(second, (EXTRA, count))


def unpack(packed_ref):
    count = packed_ref.shape[1]
    half = count // 2
    upper, diagonal, left = half_masks(half, count)
    top = packed_ref[:half]
    second = packed_ref[half:half + 1]
    mirror = jnp.swapaxes(jnp.concatenate([top, jnp.zeros_like(top)], axis=0), 0, 1)
    first = jnp.where(upper, mirror[:half], top)
    last = jnp.where(diagonal, second, jnp.where(upper, top, mirror[:half]))
    last = jnp.where(left, mirror[half:], pltpu.roll(last, half, 1))
    return jnp.concatenate([first, last], axis=0)


def base_kernel(scale, features, near_ref, far_ref, base_ref):
    count = base_ref.shape[0]
    coeff = scale * 4.0 * covariance_weight / (features * (count - 1))
    centred = centre(whole(near_ref, far_ref))
    variance = jnp.sum(centred * centred, axis=0, keepdims=True) / (count - 1)
    spread = jnp.sqrt(variance + epsilon_var)
    wide = centred.astype(BF16).astype(F32)
    diag_cov = jnp.sum(wide * wide, axis=0, keepdims=True) / (count - 1)
    var_coeff = jnp.where(
        spread < 1.0, -scale * variance_weight / (features * (count - 1)) / spread, 0.0
    )
    base_ref[...] = var_coeff * centred - coeff * diag_cov * wide


def grads_kernel(own, scale, features, me_ref, packed_ref, c_ref, near_ref, far_ref, other_ref,
                 base_ref, w_ref, grad_ref, send_ref, rel_ref):
    me = me_ref[0]
    count, width = c_ref.shape
    devices = count // own
    rest = unpack(packed_ref)
    through = 0.0
    for _ in range(2):
        piece = rest.astype(BF16)
        rest = rest - piece.astype(F32)
        through = through + jnp.dot(piece, c_ref[...], preferred_element_type=F32)
    for device in range(devices):
        rel_ref[slot_of(device, me, devices // QUAD)] = through[device * own:(device + 1) * own]
    coeff = scale * 4.0 * covariance_weight / (features * (count - 1))
    other = other_ref[...].reshape(devices // 2, 2, own, width)
    other = jnp.concatenate([other[:, 1:], other[:, :1]], axis=1).reshape(count, width)
    gap = whole(near_ref, far_ref) - other
    inv_term = gap * (scale * 2.0 * invariance_weight / (count * features))
    through = rel_ref[...].reshape(count, width)
    grad = (inv_term + base_ref[...] + through * (coeff / (count - 1))).astype(BF16)
    grad_ref[...] = grad
    send_ref[...] = nt_dot(grad[count // 2:], w_ref[...]).astype(BF16)


def join_kernel(me_ref, own_ref, other_ref, out_ref):
    second = me_ref[0] % 2 == 1
    own, other = own_ref[...], other_ref[...]
    out_ref[:, 0, :] = jnp.where(second, other, own)
    out_ref[:, 1, :] = jnp.where(second, own, other)


def weight_operands(rows_ref, rows_core_ref, grad_ref, grad_core_ref):
    block = grad_core_ref.shape[1]
    rows = jnp.concatenate([rows_ref[...], rows_core_ref[...]], axis=0)
    return rows, jnp.concatenate([grad_ref[:, :block], grad_core_ref[...]], axis=0)


def tn_dot(a, b):
    return lax.dot_general(a, b, (((0,), (0,)), ((), ())), preferred_element_type=F32)


def weight_kernel(*refs):
    part = tn_dot(*weight_operands(*refs[:4]))
    refs[-1][...] = part + refs[4][...] if len(refs) > 5 else part


def last_weight_kernel(*refs):
    *operand_refs, earlier_ref, out_ref, sum_ref, sems = refs
    rows, grads = weight_operands(*operand_refs)
    bands, height, _ = sum_ref.shape
    copies = []
    for i in range(bands):
        band = slice(i * height, (i + 1) * height)
        sum_ref[i] = tn_dot(rows[:, band], grads) + earlier_ref[band]
        copies.append(pltpu.make_async_copy(sum_ref.at[i], out_ref.at[pl.ds(i * height, height)], sems.at[i]))
        copies[-1].start()
    for copy in copies:
        copy.wait()


def call(kernel, out_shape, specs, scratch=(), place=VMEM):
    return pl.pallas_call(
        kernel,
        out_shape=out_shape,
        in_specs=specs,
        out_specs=jax.tree.map(lambda _: place, out_shape),
        scratch_shapes=list(scratch),
        compiler_params=pltpu.CompilerParams(vmem_limit_bytes=32 * 1024 * 1024),
    )


def shards(images, weight):
    groups = lax.axis_size("rep")
    owners = lax.axis_size("dp")
    own, views, depth = images.shape
    block = weight.shape[1]
    width = 2 * block
    features = block * owners
    count = own * owners
    half = count // 2
    lot = 2 * own
    outer = owners // QUAD
    scale = loss_scale / groups
    position = lax.axis_index("dp")
    me = position.reshape(1)
    struct = jax.ShapeDtypeStruct

    def over_rep(array):
        return [
            lax.ppermute(array, "rep", [(i, (i + shift) % groups) for i in range(groups)])
            for shift in range(1, groups)
        ]

    def matmul(rows, matrix):
        return jnp.dot(rows, matrix, preferred_element_type=F32)

    given = swap(images, "dp", CORE)
    weight_core = swap(weight, "dp", CORE)
    mine = call(split_kernel, struct((lot, depth), BF16), [SMEM] + [VMEM] * 2)(me, images, given)
    column = [swap(mine, "dp", high * QUAD) for high in range(1, outer)]
    wide = jnp.concatenate([weight, weight_core], axis=1)
    column, wide = lax.optimization_barrier((column, wide))
    column = jnp.concatenate([mine] + column, axis=0)
    across = swap(column, "dp", ACROSS)
    near = matmul(column, wide)
    near, across = lax.optimization_barrier((near, across))
    far = matmul(across, wide)

    c, packed = call(
        functools.partial(gram_kernel, own),
        (struct((count, width), BF16), struct((half + EXTRA, count), F32)),
        [SMEM] + [VMEM] * 2,
        [pltpu.VMEM((owners, own, width), F32)],
    )(me, near, far)

    along, beside, corner = (swap(packed, "dp", bits) for bits in (ACROSS, QUAD, ACROSS | QUAD))
    packed = (packed + along) + (beside + corner)
    packed, near_late, far_late, rows = lax.optimization_barrier(
        (packed, near, far, jnp.concatenate([column, across], axis=0))
    )
    rows_core = swap(rows, "dp", CORE)
    base = call(
        functools.partial(base_kernel, scale, features), struct((count, width), F32), [VMEM] * 2
    )(near_late, far_late)
    base, sent = lax.optimization_barrier((base, rows))
    rows_others = over_rep(sent)
    other = matmul(rows_core, wide)
    bit = 2 * QUAD
    while bit < owners:
        received = swap(packed, "dp", bit)
        received, other, base = lax.optimization_barrier((received, other, base))
        packed = packed + received
        bit *= 2

    grad, send = call(
        functools.partial(grads_kernel, own, scale, features),
        (struct((count, width), BF16), struct((half, depth), BF16)),
        [SMEM] + [VMEM] * 7,
        [pltpu.VMEM((owners, own, width), F32)],
    )(me, packed, c, near, far, other, base, wide)

    def weight_part(*operands):
        return call(weight_kernel, struct((depth, block), F32), [VMEM] * len(operands))(*operands)

    received = swap(send, "dp", ACROSS)
    keep = nt_dot(grad[:half], wide)
    keep, grad = lax.optimization_barrier((keep, grad))
    grad_others = over_rep(grad)
    grad_core = swap(grad[:, block:], "dp", CORE)
    keep = (keep + received.astype(F32)).reshape(outer, lot, depth)
    received = [
        swap(keep[high].astype(BF16), "dp", high * QUAD) for high in range(1, outer)
    ]
    grad, grad_others = lax.optimization_barrier((grad, grad_others))
    weight_grad = weight_part(rows, rows_core, grad, grad_core)
    received, weight_grad = lax.optimization_barrier((received, weight_grad))
    total = keep[0]
    for array in received:
        total = total + array.astype(F32)
    view_other = swap(total[own:], "dp", CORE)
    height = min(depth, 256)
    for left, (theirs, theirs_grad) in enumerate(zip(rows_others, grad_others), 2 - groups):
        operands = [
            theirs, swap(theirs, "dp", CORE),
            theirs_grad, swap(theirs_grad[:, block:], "dp", CORE), weight_grad,
        ]
        if left < 0:
            weight_grad = weight_part(*operands)
        else:
            weight_grad = call(
                last_weight_kernel, struct((depth, block), F32), [VMEM] * 5,
                [
                    pltpu.VMEM((depth // height, height, block), F32),
                    pltpu.SemaphoreType.DMA((depth // height,)),
                ],
                pl.BlockSpec(memory_space=pl.ANY),
            )(*operands)
    view_other, weight_grad = lax.optimization_barrier((view_other, weight_grad))
    image_grad = call(join_kernel, struct((own, views, depth), F32), [SMEM] + [VMEM] * 2)(
        me, total[:own], view_other
    )
    return (image_grad, weight_grad)


def solution(mesh):
    return jax.shard_map(
        shards,
        mesh=mesh,
        in_specs=(P(("rep", "dp"), None, None), P(None, "dp")),
        out_specs=(P(("rep", "dp"), None, None), P(None, "dp")),
        check_vma=False,
    )
```

profile of v0, /device:TPU:0, one launch (start us, length us, event | category | flops | bytes accessed | tf_op | source)
XLA Modules:
  0.0 51.2 jit_solution(15798864771936466540)
XLA Ops:
  0.6 0.5 %collective-permute-start.4 = (bf16[1280,512]{1,0:T(8,128)(2,1)}, bf16[1280,512]{1,0:T(8,128)(2,1)S(1)}, u32[]{:S(2)}, u32[]{:S(2)}) collective-permute-start(bf16[1280,512]{1,0:T(8,128)(2,1)} %param.3), channel_id=1, source_target_pairs={{0,1},{1,0},{2,3},{3,2},{4,5},{5,4},{6,7},{7,6},{8,9},{9,8},{10,11... | collective-permute-start | bytes 3932168 | tf_op jit(solution)/shard_map/ppermute | solution.py:25
  1.2 2.9 %collective-permute-done.refs_1_ = bf16[8,2,1280]{2,1,0:T(2,128)(2,1)S(1)} collective-permute-done((bf16[8,2,1280]{2,1,0:T(2,128)(2,1)}, bf16[8,2,1280]{2,1,0:T(2,128)(2,1)S(1)}, u32[]{:S(2)}, u32[]{:S(2)}) %collective-permute-start) | collective-permute-done | bytes 40992 | tf_op jit(solution)/shard_map/ppermute | solution.py:25
  4.1 0.8 %copy-done = bf16[8,2,1280]{2,1,0:T(2,128)(2,1)S(1)} copy-done((bf16[8,2,1280]{2,1,0:T(2,128)(2,1)S(1)}, bf16[8,2,1280]{2,1,0:T(2,128)(2,1)}, u32[]{:S(2)}) %copy-start) | copy-done | bytes 40984
  5.0 5.0 %collective-permute-start.3 = (bf16[16,1280]{1,0:T(8,128)(2,1)S(1)}, bf16[16,1280]{1,0:T(8,128)(2,1)S(1)}, u32[]{:S(2)}, u32[]{:S(2)}) collective-permute-start(bf16[16,1280]{1,0:T(8,128)(2,1)S(1)} %shard_map.41), channel_id=1, source_target_pairs={{0,12},{1,13},{2,14},{3,15},{4,8},{5,9},{6,10},{7,11},{8,4},{9,5},... | collective-permute-start | bytes 122888 | tf_op jit(solution)/shard_map/ppermute | solution.py:25
  10.0 0.6 %collective-permute-start.1 = (bf16[16,1280]{1,0:T(8,128)(2,1)S(1)}, bf16[16,1280]{1,0:T(8,128)(2,1)S(1)}, u32[]{:S(2)}, u32[]{:S(2)}) collective-permute-start(bf16[16,1280]{1,0:T(8,128)(2,1)S(1)} %shard_map.41), channel_id=1, source_target_pairs={{0,4},{1,5},{2,6},{3,7},{4,0},{5,1},{6,2},{7,3},{8,12},{9,13},{10,... | collective-permute-start | bytes 122888 | tf_op jit(solution)/shard_map/ppermute | solution.py:25
  10.7 1.7 %pad_maximum_fusion.w_ref = bf16[1280,1024]{1,0:T(8,128)(2,1)S(1)} fusion(bf16[1280,512]{1,0:T(8,128)(2,1)S(1)} %collective-permute-done.4, bf16[1280,512]{1,0:T(8,128)(2,1)} %param.3), kind=kLoop, calls=%fused_computation | loop fusion | flops 5242880 | bytes 5242880 | tf_op jit(solution)/shard_map/concatenate | solution.py:207
  12.4 2.5 %collective-permute-done.2 = bf16[16,1280]{1,0:T(8,128)(2,1)S(1)} collective-permute-done((bf16[16,1280]{1,0:T(8,128)(2,1)S(1)}, bf16[16,1280]{1,0:T(8,128)(2,1)S(1)}, u32[]{:S(2)}, u32[]{:S(2)}) %collective-permute-start.2) | collective-permute-done | bytes 40992 | tf_op jit(solution)/shard_map/ppermute | solution.py:25
  15.0 0.6 %fusion.4.near_ref = f32[64,1024]{1,0:T(8,128)S(1)} fusion(bf16[1280,1024]{1,0:T(8,128)(2,1)S(1)} %pad_maximum_fusion.w_ref, bf16[16,1280]{1,0:T(8,128)(2,1)S(1)} %collective-permute-done.3, bf16[16,1280]{1,0:T(8,128)(2,1)S(1)} %collective-permute-done.2, bf16[16,1280]{1,0:T(8,128)(2,1)S(1)} %collective-permute-done.1, bf16[16,1280]{1,0:T(8,128)(2,1)S(1)} %shard_map.41), kind=kOutput, calls=%fused_computation.14 | convolution fusion | flops 168427520 | bytes 3047424 | tf_op jit(solution)/shard_map/dot_general | solution.py:201
  15.5 1.6 %collective-permute-start.5 = (bf16[64,1280]{1,0:T(8,128)(2,1)S(1)}, bf16[64,1280]{1,0:T(8,128)(2,1)S(1)}, u32[]{:S(2)}, u32[]{:S(2)}) collective-permute-start(bf16[64,1280]{1,0:T(8,128)(2,1)S(1)} %pad_maximum_fusion.1), channel_id=1, source_target_pairs={{0,2},{1,3},{2,0},{3,1},{4,6},{5,7},{6,4},{7,5},{8,10},{9,11},{10,... | collective-permute-start | bytes 491528 | tf_op jit(solution)/shard_map/ppermute | solution.py:25
  17.1 3.8 %collective-permute-done.5 = bf16[64,1280]{1,0:T(8,128)(2,1)S(1)} collective-permute-done((bf16[64,1280]{1,0:T(8,128)(2,1)S(1)}, bf16[64,1280]{1,0:T(8,128)(2,1)S(1)}, u32[]{:S(2)}, u32[]{:S(2)}) %collective-permute-start.5) | collective-permute-done | bytes 163872 | tf_op jit(solution)/shard_map/ppermute | solution.py:25
  20.9 0.6 %fusion.8.far_ref = f32[64,1024]{1,0:T(8,128)S(1)} fusion(bf16[64,1280]{1,0:T(8,128)(2,1)S(1)} %collective-permute-done.5, bf16[1280,1024]{1,0:T(8,128)(2,1)S(1)} %pad_maximum_fusion.w_ref), kind=kOutput, calls=%fused_computation.18 | convolution fusion | flops 167772160 | bytes 3047424 | tf_op jit(solution)/shard_map/dot_general | solution.py:201
  21.9 1.4 %collective-permute-start.8 = (f32[72,128]{1,0:T(8,128)S(1)}, f32[72,128]{1,0:T(8,128)S(1)}, u32[]{:S(2)}, u32[]{:S(2)}) collective-permute-start(f32[72,128]{1,0:T(8,128)S(1)} %get-tuple-element.37), channel_id=1, source_target_pairs={{0,6},{1,7},{2,4},{3,5},{4,2},{5,3},{6,0},{7,1},{8,14},{9,15},{10,... | collective-permute-start | bytes 110600 | tf_op jit(solution)/shard_map/ppermute | solution.py:25
  23.3 1.6 %collective-permute-start.7 = (f32[72,128]{1,0:T(8,128)S(1)}, f32[72,128]{1,0:T(8,128)S(1)}, u32[]{:S(2)}, u32[]{:S(2)}) collective-permute-start(f32[72,128]{1,0:T(8,128)S(1)} %get-tuple-element.37), channel_id=1, source_target_pairs={{0,4},{1,5},{2,6},{3,7},{4,0},{5,1},{6,2},{7,3},{8,12},{9,13},{10,... | collective-permute-start | bytes 110600 | tf_op jit(solution)/shard_map/ppermute | solution.py:25
  24.9 0.5 %collective-permute-start.6 = (f32[72,128]{1,0:T(8,128)S(1)}, f32[72,128]{1,0:T(8,128)S(1)}, u32[]{:S(2)}, u32[]{:S(2)}) collective-permute-start(f32[72,128]{1,0:T(8,128)S(1)} %get-tuple-element.37), channel_id=1, source_target_pairs={{0,2},{1,3},{2,0},{3,1},{4,6},{5,7},{6,4},{7,5},{8,10},{9,11},{10,... | collective-permute-start | bytes 110600 | tf_op jit(solution)/shard_map/ppermute | solution.py:25
  25.5 1.4 %collective-permute-done.8 = f32[72,128]{1,0:T(8,128)S(1)} collective-permute-done((f32[72,128]{1,0:T(8,128)S(1)}, f32[72,128]{1,0:T(8,128)S(1)}, u32[]{:S(2)}, u32[]{:S(2)}) %collective-permute-start.8) | collective-permute-done | bytes 36896 | tf_op jit(solution)/shard_map/ppermute | solution.py:25
  27.3 1.6 %collective-permute-done.6 = f32[72,128]{1,0:T(8,128)S(1)} collective-permute-done((f32[72,128]{1,0:T(8,128)S(1)}, f32[72,128]{1,0:T(8,128)S(1)}, u32[]{:S(2)}, u32[]{:S(2)}) %collective-permute-start.6) | collective-permute-done | bytes 36896 | tf_op jit(solution)/shard_map/ppermute | solution.py:25
  29.0 2.1 %collective-permute-start.9 = (f32[72,128]{1,0:T(8,128)S(1)}, f32[72,128]{1,0:T(8,128)S(1)}, u32[]{:S(2)}, u32[]{:S(2)}) collective-permute-start(f32[72,128]{1,0:T(8,128)S(1)} %add_add_fusion), channel_id=1, source_target_pairs={{0,8},{1,9},{2,10},{3,11},{4,12},{5,13},{6,14},{7,15},{8,0},{9,1},... | collective-permute-start | bytes 110600 | tf_op jit(solution)/shard_map/ppermute | solution.py:25
  31.3 1.6 %collective-permute-start.18 = (bf16[128,1280]{1,0:T(8,128)(2,1)S(1)}, bf16[128,1280]{1,0:T(8,128)(2,1)S(1)}, u32[]{:S(2)}, u32[]{:S(2)}) collective-permute-start(bf16[128,1280]{1,0:T(8,128)(2,1)S(1)} %constant_dynamic-update-slice_fusion.refs_0_), channel_id=1, source_target_pairs={{0,16},{16,0},{1,17},{17,1},{2,18},{18,2},{3,19},{19,3},{4,20},{20... | collective-permute-start | bytes 983048 | tf_op jit(solution)/shard_map/ppermute | solution.py:196
  32.9 0.5 fusion.9.other_ref
  33.4 1.0 %collective-permute-done.9 = f32[72,128]{1,0:T(8,128)S(1)} collective-permute-done((f32[72,128]{1,0:T(8,128)S(1)}, f32[72,128]{1,0:T(8,128)S(1)}, u32[]{:S(2)}, u32[]{:S(2)}) %collective-permute-start.9) | collective-permute-done | bytes 36896 | tf_op jit(solution)/shard_map/ppermute | solution.py:25
  34.5 1.5 %shard_map.44 = (bf16[128,1024]{1,0:T(8,128)(2,1)S(1)}, bf16[64,1280]{1,0:T(8,128)(2,1)S(1)}) custom-call(s32[1]{0:T(128)} %bitcast.me_ref, f32[72,128]{1,0:T(8,128)S(1)} %add.27.packed_ref, bf16[128,1024]{1,0:T(8,128)(2,1)S(1)} %get-tuple-element.44.c_ref, f32[64,1024]{1,0:T(8,128)S(1)} %fusion.4.near_ref, f32[64,1024]{1,0:T(8,128)S(1)} %fusion.8.far_ref, ...), custom_call_target="tpu_custom_call" | custom-call | tf_op jit(solution)/shard_map/pallas_call | solution.py:241
  35.9 0.6 %collective-permute-start.11 = (bf16[64,1280]{1,0:T(8,128)(2,1)S(1)}, bf16[64,1280]{1,0:T(8,128)(2,1)S(1)}, u32[]{:S(2)}, u32[]{:S(2)}) collective-permute-start(bf16[64,1280]{1,0:T(8,128)(2,1)S(1)} %get-tuple-element.49), channel_id=1, source_target_pairs={{0,2},{1,3},{2,0},{3,1},{4,6},{5,7},{6,4},{7,5},{8,10},{9,11},{10,... | collective-permute-start | bytes 491528 | tf_op jit(solution)/shard_map/ppermute | solution.py:25
  36.5 0.9 %fusion = f32[64,1280]{1,0:T(8,128)S(1)} fusion(bf16[1280,1024]{1,0:T(8,128)(2,1)S(1)} %pad_maximum_fusion.w_ref, bf16[128,1024]{1,0:T(8,128)(2,1)S(1)} %get-tuple-element.51.refs_2_), kind=kOutput, calls=%fused_computation.3 | convolution fusion | flops 167772160 | bytes 3080192 | tf_op jit(solution)/shard_map/dot_general | solution.py:39
  37.4 1.6 %collective-permute-start.15 = (bf16[128,1024]{1,0:T(8,128)(2,1)S(1)}, bf16[128,1024]{1,0:T(8,128)(2,1)S(1)}, u32[]{:S(2)}, u32[]{:S(2)}) collective-permute-start(bf16[128,1024]{1,0:T(8,128)(2,1)S(1)} %get-tuple-element.51.refs_2_), channel_id=1, source_target_pairs={{0,16},{16,0},{1,17},{17,1},{2,18},{18,2},{3,19},{19,3},{4,20},{20... | collective-permute-start | bytes 786440 | tf_op jit(solution)/shard_map/ppermute | solution.py:196
  39.0 3.0 %collective-permute-done.11 = bf16[64,1280]{1,0:T(8,128)(2,1)S(1)} collective-permute-done((bf16[64,1280]{1,0:T(8,128)(2,1)S(1)}, bf16[64,1280]{1,0:T(8,128)(2,1)S(1)}, u32[]{:S(2)}, u32[]{:S(2)}) %collective-permute-start.11) | collective-permute-done | bytes 163872 | tf_op jit(solution)/shard_map/ppermute | solution.py:25
  42.1 0.6 %collective-permute-start.14 = (bf16[16,1280]{1,0:T(8,128)(2,1)S(1)}, bf16[16,1280]{1,0:T(8,128)(2,1)S(1)}, u32[]{:S(2)}, u32[]{:S(2)}) collective-permute-start(bf16[16,1280]{1,0:T(8,128)(2,1)S(1)} %get-tuple-element.62), channel_id=1, source_target_pairs={{0,12},{1,13},{2,14},{3,15},{4,8},{5,9},{6,10},{7,11},{8,4},{9,5},... | collective-permute-start | bytes 122888 | tf_op jit(solution)/shard_map/ppermute | solution.py:25
  43.0 3.5 %collective-permute-start.12 = (bf16[16,1280]{1,0:T(8,128)(2,1)S(1)}, bf16[16,1280]{1,0:T(8,128)(2,1)S(1)}, u32[]{:S(2)}, u32[]{:S(2)}) collective-permute-start(bf16[16,1280]{1,0:T(8,128)(2,1)S(1)} %get-tuple-element.64), channel_id=1, source_target_pairs={{0,4},{1,5},{2,6},{3,7},{4,0},{5,1},{6,2},{7,3},{8,12},{9,13},{10,... | collective-permute-start | bytes 122888 | tf_op jit(solution)/shard_map/ppermute | solution.py:25
  46.8 0.6 %collective-permute-start.20 = (bf16[128,512]{1,0:T(8,128)(2,1)S(1)}, bf16[128,512]{1,0:T(8,128)(2,1)S(1)}, u32[]{:S(2)}, u32[]{:S(2)}) collective-permute-start(bf16[128,512]{1,0:T(8,128)(2,1)S(1)} %slice.42), channel_id=1, source_target_pairs={{0,1},{1,0},{2,3},{3,2},{4,5},{5,4},{6,7},{7,6},{8,9},{9,8},{10,11... | collective-permute-start | bytes 393224 | tf_op jit(solution)/shard_map/ppermute | solution.py:25
  47.4 0.5 %shard_map.45.refs_4_ = f32[1280,512]{1,0:T(8,128)S(1)} custom-call(bf16[128,1280]{1,0:T(8,128)(2,1)S(1)} %constant_dynamic-update-slice_fusion.refs_0_, bf16[128,1280]{1,0:T(8,128)(2,1)S(1)} %collective-permute-done.10.refs_1_, bf16[128,1024]{1,0:T(8,128)(2,1)S(1)} %get-tuple-element.51.refs_2_, bf16[128,512]{1,0:T(8,128)(2,1)S(1)} %collective-permute-done.16.refs_3_), custom_call_target="tpu_custom_call" | custom-call | tf_op jit(solution)/shard_map/pallas_call | solution.py:249
  48.1 0.5 collective-permute-done.13
  48.7 1.8 %shard_map.46 = f32[1280,512]{1,0:T(8,128)} custom-call(bf16[128,1280]{1,0:T(8,128)(2,1)S(1)} %collective-permute-done.18.refs_0_, bf16[128,1280]{1,0:T(8,128)(2,1)S(1)} %collective-permute-done.19.refs_1_, bf16[128,1024]{1,0:T(8,128)(2,1)S(1)} %collective-permute-done.15.refs_2_, bf16[128,512]{1,0:T(8,128)(2,1)S(1)} %collective-permute-done.20.refs_3_, ...), custom_call_target="tpu_custom_call" | custom-call | tf_op jit(solution)/shard_map/pallas_call | solution.py:276
  50.5 0.7 %shard_map.47 = f32[8,2,1280]{2,1,0:T(2,128)} custom-call(s32[1]{0:T(128)} %bitcast.me_ref, f32[8,1280]{1,0:T(8,128)S(1)} %get-tuple-element.66.own_ref, f32[8,1280]{1,0:T(8,128)S(1)} %collective-permute-done.17.other_ref), custom_call_target="tpu_custom_call" | custom-call | tf_op jit(solution)/shard_map/pallas_call | solution.py:285
  (38 shorter events, 2.3 us)
Async XLA Ops:
  0.6 10.0 %collective-permute-start.4 = (bf16[1280,512]{1,0:T(8,128)(2,1)}, bf16[1280,512]{1,0:T(8,128)(2,1)S(1)}, u32[]{:S(2)}, u32[]{:S(2)}) collective-permute-start(bf16[1280,512]{1,0:T(8,128)(2,1)} %param.3), channel_id=1, source_target_pairs={{0,1},{1,0},{2,3},{3,2},{4,5},{5,4},{6,7},{7,6},{8,9},{9,8},{10,11... | collective-permute-start | bytes 3932168 | tf_op jit(solution)/shard_map/ppermute | solution.py:25
  1.1 2.9 %collective-permute-start = (bf16[8,2,1280]{2,1,0:T(2,128)(2,1)}, bf16[8,2,1280]{2,1,0:T(2,128)(2,1)S(1)}, u32[]{:S(2)}, u32[]{:S(2)}) collective-permute-start(bf16[8,2,1280]{2,1,0:T(2,128)(2,1)} %refs_0_.1), channel_id=1, source_target_pairs={{0,1},{1,0},{2,3},{3,2},{4,5},{5,4},{6,7},{7,6},{8,9},{9,8},{10,11... | collective-permute-start | bytes 122888 | tf_op jit(solution)/shard_map/ppermute | solution.py:25
  4.1 0.8 %copy-start = (bf16[8,2,1280]{2,1,0:T(2,128)(2,1)S(1)}, bf16[8,2,1280]{2,1,0:T(2,128)(2,1)}, u32[]{:S(2)}) copy-start(bf16[8,2,1280]{2,1,0:T(2,128)(2,1)} %refs_0_.1) | copy-start | bytes 122884
  5.0 7.4 %collective-permute-start.3 = (bf16[16,1280]{1,0:T(8,128)(2,1)S(1)}, bf16[16,1280]{1,0:T(8,128)(2,1)S(1)}, u32[]{:S(2)}, u32[]{:S(2)}) collective-permute-start(bf16[16,1280]{1,0:T(8,128)(2,1)S(1)} %shard_map.41), channel_id=1, source_target_pairs={{0,12},{1,13},{2,14},{3,15},{4,8},{5,9},{6,10},{7,11},{8,4},{9,5},... | collective-permute-start | bytes 122888 | tf_op jit(solution)/shard_map/ppermute | solution.py:25
  10.0 4.9 %collective-permute-start.2 = (bf16[16,1280]{1,0:T(8,128)(2,1)S(1)}, bf16[16,1280]{1,0:T(8,128)(2,1)S(1)}, u32[]{:S(2)}, u32[]{:S(2)}) collective-permute-start(bf16[16,1280]{1,0:T(8,128)(2,1)S(1)} %shard_map.41), channel_id=1, source_target_pairs={{0,8},{1,9},{2,10},{3,11},{4,12},{5,13},{6,14},{7,15},{8,0},{9,1},... | collective-permute-start | bytes 122888 | tf_op jit(solution)/shard_map/ppermute | solution.py:25
  10.0 4.9 %collective-permute-start.1 = (bf16[16,1280]{1,0:T(8,128)(2,1)S(1)}, bf16[16,1280]{1,0:T(8,128)(2,1)S(1)}, u32[]{:S(2)}, u32[]{:S(2)}) collective-permute-start(bf16[16,1280]{1,0:T(8,128)(2,1)S(1)} %shard_map.41), channel_id=1, source_target_pairs={{0,4},{1,5},{2,6},{3,7},{4,0},{5,1},{6,2},{7,3},{8,12},{9,13},{10,... | collective-permute-start | bytes 122888 | tf_op jit(solution)/shard_map/ppermute | solution.py:25
  15.5 5.4 %collective-permute-start.5 = (bf16[64,1280]{1,0:T(8,128)(2,1)S(1)}, bf16[64,1280]{1,0:T(8,128)(2,1)S(1)}, u32[]{:S(2)}, u32[]{:S(2)}) collective-permute-start(bf16[64,1280]{1,0:T(8,128)(2,1)S(1)} %pad_maximum_fusion.1), channel_id=1, source_target_pairs={{0,2},{1,3},{2,0},{3,1},{4,6},{5,7},{6,4},{7,5},{8,10},{9,11},{10,... | collective-permute-start | bytes 491528 | tf_op jit(solution)/shard_map/ppermute | solution.py:25
  21.9 4.9 %collective-permute-start.8 = (f32[72,128]{1,0:T(8,128)S(1)}, f32[72,128]{1,0:T(8,128)S(1)}, u32[]{:S(2)}, u32[]{:S(2)}) collective-permute-start(f32[72,128]{1,0:T(8,128)S(1)} %get-tuple-element.37), channel_id=1, source_target_pairs={{0,6},{1,7},{2,4},{3,5},{4,2},{5,3},{6,0},{7,1},{8,14},{9,15},{10,... | collective-permute-start | bytes 110600 | tf_op jit(solution)/shard_map/ppermute | solution.py:25
  23.3 4.0 %collective-permute-start.7 = (f32[72,128]{1,0:T(8,128)S(1)}, f32[72,128]{1,0:T(8,128)S(1)}, u32[]{:S(2)}, u32[]{:S(2)}) collective-permute-start(f32[72,128]{1,0:T(8,128)S(1)} %get-tuple-element.37), channel_id=1, source_target_pairs={{0,4},{1,5},{2,6},{3,7},{4,0},{5,1},{6,2},{7,3},{8,12},{9,13},{10,... | collective-permute-start | bytes 110600 | tf_op jit(solution)/shard_map/ppermute | solution.py:25
  24.9 4.0 %collective-permute-start.6 = (f32[72,128]{1,0:T(8,128)S(1)}, f32[72,128]{1,0:T(8,128)S(1)}, u32[]{:S(2)}, u32[]{:S(2)}) collective-permute-start(f32[72,128]{1,0:T(8,128)S(1)} %get-tuple-element.37), channel_id=1, source_target_pairs={{0,2},{1,3},{2,0},{3,1},{4,6},{5,7},{6,4},{7,5},{8,10},{9,11},{10,... | collective-permute-start | bytes 110600 | tf_op jit(solution)/shard_map/ppermute | solution.py:25
  28.9 4.0 %collective-permute-start.10 = (bf16[128,1280]{1,0:T(8,128)(2,1)S(1)}, bf16[128,1280]{1,0:T(8,128)(2,1)S(1)}, u32[]{:S(2)}, u32[]{:S(2)}) collective-permute-start(bf16[128,1280]{1,0:T(8,128)(2,1)S(1)} %constant_dynamic-update-slice_fusion.refs_0_), channel_id=1, source_target_pairs={{0,1},{1,0},{2,3},{3,2},{4,5},{5,4},{6,7},{7,6},{8,9},{9,8},{10,11... | collective-permute-start | bytes 983048 | tf_op jit(solution)/shard_map/ppermute | solution.py:25
  29.0 5.5 %collective-permute-start.9 = (f32[72,128]{1,0:T(8,128)S(1)}, f32[72,128]{1,0:T(8,128)S(1)}, u32[]{:S(2)}, u32[]{:S(2)}) collective-permute-start(f32[72,128]{1,0:T(8,128)S(1)} %add_add_fusion), channel_id=1, source_target_pairs={{0,8},{1,9},{2,10},{3,11},{4,12},{5,13},{6,14},{7,15},{8,0},{9,1},... | collective-permute-start | bytes 110600 | tf_op jit(solution)/shard_map/ppermute | solution.py:25
  31.3 11.8 %collective-permute-start.18 = (bf16[128,1280]{1,0:T(8,128)(2,1)S(1)}, bf16[128,1280]{1,0:T(8,128)(2,1)S(1)}, u32[]{:S(2)}, u32[]{:S(2)}) collective-permute-start(bf16[128,1280]{1,0:T(8,128)(2,1)S(1)} %constant_dynamic-update-slice_fusion.refs_0_), channel_id=1, source_target_pairs={{0,16},{16,0},{1,17},{17,1},{2,18},{18,2},{3,19},{19,3},{4,20},{20... | collective-permute-start | bytes 983048 | tf_op jit(solution)/shard_map/ppermute | solution.py:196
  35.9 6.2 %collective-permute-start.11 = (bf16[64,1280]{1,0:T(8,128)(2,1)S(1)}, bf16[64,1280]{1,0:T(8,128)(2,1)S(1)}, u32[]{:S(2)}, u32[]{:S(2)}) collective-permute-start(bf16[64,1280]{1,0:T(8,128)(2,1)S(1)} %get-tuple-element.49), channel_id=1, source_target_pairs={{0,2},{1,3},{2,0},{3,1},{4,6},{5,7},{6,4},{7,5},{8,10},{9,11},{10,... | collective-permute-start | bytes 491528 | tf_op jit(solution)/shard_map/ppermute | solution.py:25
  37.4 9.3 %collective-permute-start.15 = (bf16[128,1024]{1,0:T(8,128)(2,1)S(1)}, bf16[128,1024]{1,0:T(8,128)(2,1)S(1)}, u32[]{:S(2)}, u32[]{:S(2)}) collective-permute-start(bf16[128,1024]{1,0:T(8,128)(2,1)S(1)} %get-tuple-element.51.refs_2_), channel_id=1, source_target_pairs={{0,16},{16,0},{1,17},{17,1},{2,18},{18,2},{3,19},{19,3},{4,20},{20... | collective-permute-start | bytes 786440 | tf_op jit(solution)/shard_map/ppermute | solution.py:196
  39.0 7.8 %collective-permute-start.16 = (bf16[128,512]{1,0:T(8,128)(2,1)S(1)}, bf16[128,512]{1,0:T(8,128)(2,1)S(1)}, u32[]{:S(2)}, u32[]{:S(2)}) collective-permute-start(bf16[128,512]{1,0:T(8,128)(2,1)S(1)} %slice.39), channel_id=1, source_target_pairs={{0,1},{1,0},{2,3},{3,2},{4,5},{5,4},{6,7},{7,6},{8,9},{9,8},{10,11... | collective-permute-start | bytes 393224 | tf_op jit(solution)/shard_map/ppermute | solution.py:25
  42.1 6.0 %collective-permute-start.14 = (bf16[16,1280]{1,0:T(8,128)(2,1)S(1)}, bf16[16,1280]{1,0:T(8,128)(2,1)S(1)}, u32[]{:S(2)}, u32[]{:S(2)}) collective-permute-start(bf16[16,1280]{1,0:T(8,128)(2,1)S(1)} %get-tuple-element.62), channel_id=1, source_target_pairs={{0,12},{1,13},{2,14},{3,15},{4,8},{5,9},{6,10},{7,11},{8,4},{9,5},... | collective-permute-start | bytes 122888 | tf_op jit(solution)/shard_map/ppermute | solution.py:25
  42.8 5.8 %collective-permute-start.13 = (bf16[16,1280]{1,0:T(8,128)(2,1)S(1)}, bf16[16,1280]{1,0:T(8,128)(2,1)S(1)}, u32[]{:S(2)}, u32[]{:S(2)}) collective-permute-start(bf16[16,1280]{1,0:T(8,128)(2,1)S(1)} %get-tuple-element.63), channel_id=1, source_target_pairs={{0,8},{1,9},{2,10},{3,11},{4,12},{5,13},{6,14},{7,15},{8,0},{9,1},... | collective-permute-start | bytes 122888 | tf_op jit(solution)/shard_map/ppermute | solution.py:25
  43.0 5.5 %collective-permute-start.12 = (bf16[16,1280]{1,0:T(8,128)(2,1)S(1)}, bf16[16,1280]{1,0:T(8,128)(2,1)S(1)}, u32[]{:S(2)}, u32[]{:S(2)}) collective-permute-start(bf16[16,1280]{1,0:T(8,128)(2,1)S(1)} %get-tuple-element.64), channel_id=1, source_target_pairs={{0,4},{1,5},{2,6},{3,7},{4,0},{5,1},{6,2},{7,3},{8,12},{9,13},{10,... | collective-permute-start | bytes 122888 | tf_op jit(solution)/shard_map/ppermute | solution.py:25
  46.8 1.9 %collective-permute-start.19 = (bf16[128,1280]{1,0:T(8,128)(2,1)S(1)}, bf16[128,1280]{1,0:T(8,128)(2,1)S(1)}, u32[]{:S(2)}, u32[]{:S(2)}) collective-permute-start(bf16[128,1280]{1,0:T(8,128)(2,1)S(1)} %collective-permute-done.18.refs_0_), channel_id=1, source_target_pairs={{0,1},{1,0},{2,3},{3,2},{4,5},{5,4},{6,7},{7,6},{8,9},{9,8},{10,11... | collective-permute-start | bytes 983048 | tf_op jit(solution)/shard_map/ppermute | solution.py:25
  46.8 1.9 %collective-permute-start.20 = (bf16[128,512]{1,0:T(8,128)(2,1)S(1)}, bf16[128,512]{1,0:T(8,128)(2,1)S(1)}, u32[]{:S(2)}, u32[]{:S(2)}) collective-permute-start(bf16[128,512]{1,0:T(8,128)(2,1)S(1)} %slice.42), channel_id=1, source_target_pairs={{0,1},{1,0},{2,3},{3,2},{4,5},{5,4},{6,7},{7,6},{8,9},{9,8},{10,11... | collective-permute-start | bytes 393224 | tf_op jit(solution)/shard_map/ppermute | solution.py:25
  48.6 1.9 %collective-permute-start.17 = (f32[8,1280]{1,0:T(8,128)S(1)}, f32[8,1280]{1,0:T(8,128)S(1)}, u32[]{:S(2)}, u32[]{:S(2)}) collective-permute-start(f32[8,1280]{1,0:T(8,128)S(1)} %get-tuple-element.65), channel_id=1, source_target_pairs={{0,1},{1,0},{2,3},{3,2},{4,5},{5,4},{6,7},{7,6},{8,9},{9,8},{10,11... | collective-permute-start | bytes 122888 | tf_op jit(solution)/shard_map/ppermute | solution.py:25
where the time goes:
time: 51.4 us; the launch traced here: 51.2 us
  starting transfers between devices  22.4 us (44%)
  waiting for transfers between devices  17.6 us (34%)
  Pallas kernels  5.19 us (10%)
  matrix products  2.57 us (5%)
  other arithmetic  1.81 us (4%)
  local copies, waits for them, and re-layouts  0.85 us (2%)
  between operations  0.81 us (2%)
    ppermute x19, starting transfers between devices, swap(): lax.ppermute(block, axis, [(i, i ^ bits) for i in range(lax.axis_size(axi...  19.2 us
    ppermute x19, waiting for transfers between devices, swap(): lax.ppermute(block, axis, [(i, i ^ bits) for i in range(lax.axis_size(axi...  17.4 us
    ppermute x2, starting transfers between devices, over_rep(): lax.ppermute(array, 'rep', [(i, (i + shift) % groups) for i in range(grou...  3.17 us
    pallas_call x1, Pallas kernels, shards(): call(last_weight_kernel, struct((depth, block), F32), [VMEM] * 5, [pltpu....  1.79 us
    concatenate x1, other arithmetic, shards(): wide = jnp.concatenate([weight, weight_core], axis=1)  1.71 us
    dot_general x3, matrix products, matmul(): return jnp.dot(rows, matrix, preferred_element_type=F32)  1.66 us
    pallas_call x1, Pallas kernels, shards(): call(functools.partial(grads_kernel, own, scale, features), (struct((coun...  1.45 us
  transfers between devices with their start and end apart: 21, of which 11 were waited for; matrix products, arithmetic and copies ran while one was open for 6% of the time, Pallas kernels for 8%

commit v1 on v0

--- a/solution.py
+++ b/solution.py
@@ -49,12 +49,15 @@
     return jnp.concatenate([near_ref[...], far_ref[...]], axis=0)
 
 
-def split_kernel(me_ref, *refs):
-    second = me_ref[0] % 2 == 1
-    *image_refs, rows_ref = refs
-    own = image_refs[0].shape[0]
-    parts = [jnp.where(second, ref[:, 1, :], ref[:, 0, :]) for ref in image_refs]
-    rows_ref[...] = jnp.concatenate(parts, axis=0)
+def pick_kernel(me_ref, images_ref, rows_ref):
+    images = images_ref[...]
+    rows_ref[...] = jnp.where(me_ref[0] % 2 == 1, images[:, 1, :], images[:, 0, :])
+
+
+def pair_kernel(me_ref, rows_ref, images_ref, both_ref):
+    images = images_ref[...]
+    rows = jnp.where(me_ref[0] % 2 == 1, images[:, 1, :], images[:, 0, :])
+    both_ref[...] = jnp.concatenate([rows_ref[...], rows], axis=0)
 
 
 def gram_kernel(own, me_ref, near_ref, far_ref, c_ref, packed_ref, sorted_ref):
@@ -201,12 +204,14 @@
         return jnp.dot(rows, matrix, preferred_element_type=F32)
 
     given = swap(images, "dp", CORE)
-    weight_core = swap(weight, "dp", CORE)
-    mine = call(split_kernel, struct((lot, depth), BF16), [SMEM] + [VMEM] * 2)(me, images, given)
+    mine = call(pick_kernel, struct((own, depth), BF16), [SMEM, VMEM])(me, images)
+    given, mine, sent = lax.optimization_barrier((given, mine, weight))
+    weight_core = swap(sent, "dp", CORE)
+    mine = call(pair_kernel, struct((lot, depth), BF16), [SMEM] + [VMEM] * 2)(me, mine, given)
     column = [swap(mine, "dp", high * QUAD) for high in range(1, outer)]
     wide = jnp.concatenate([weight, weight_core], axis=1)
     column, wide = lax.optimization_barrier((column, wide))
-    column = jnp.concatenate([mine] + column, axis=0)
+    column = lax.optimization_barrier(jnp.concatenate([mine] + column, axis=0))
     across = swap(column, "dp", ACROSS)
     near = matmul(column, wide)
     near, across = lax.optimization_barrier((near, across))

time: 51.4 us -> 48.9 us (0.951)
  waiting for transfers between devices: 17.6 us -> 15.2 us
    ppermute x19, waiting for transfers between devices: 17.4 us -> 15.2 us  [swap(): lax.ppermute(block, axis, [(i, i ^ bits) for i in range(lax.axis_size(axi...]
  transfers between devices with their start and end apart: 21 -> 21, of which waited for: 11 -> 10; matrix products, arithmetic and copies ran while one was open for 6% -> 8% of each run, Pallas kernels for 8% -> 9%
where the time goes in v1:
time: 48.9 us; the launch traced here: 48.7 us
  starting transfers between devices  22.3 us (46%)
  waiting for transfers between devices  15.2 us (31%)
  Pallas kernels  5.22 us (11%)
  matrix products  2.54 us (5%)
  other arithmetic  1.78 us (4%)
  local copies, waits for them, and re-layouts  0.82 us (2%)
  between operations  0.8 us (2%)
    ppermute x19, starting transfers between devices, swap(): lax.ppermute(block, axis, [(i, i ^ bits) for i in range(lax.axis_size(axi...  19.2 us
    ppermute x19, waiting for transfers between devices, swap(): lax.ppermute(block, axis, [(i, i ^ bits) for i in range(lax.axis_size(axi...  15.2 us
    ppermute x2, starting transfers between devices, over_rep(): lax.ppermute(array, 'rep', [(i, (i + shift) % groups) for i in range(grou...  3.17 us
    pallas_call x1, Pallas kernels, shards(): call(last_weight_kernel, struct((depth, block), F32), [VMEM] * 5, [pltpu....  1.81 us
    concatenate x1, other arithmetic, shards(): wide = jnp.concatenate([weight, weight_core], axis=1)  1.67 us
    dot_general x3, matrix products, matmul(): return jnp.dot(rows, matrix, preferred_element_type=F32)  1.64 us
    pallas_call x1, Pallas kernels, shards(): call(functools.partial(grads_kernel, own, scale, features), (struct((coun...  1.45 us
  transfers between devices with their start and end apart: 21, of which 10 were waited for; matrix products, arithmetic and copies ran while one was open for 8% of the time, Pallas kernels for 9%

profile of v1, /device:TPU:0, one launch (start us, length us, event | category | flops | bytes accessed | tf_op | source)
XLA Modules:
  0.0 48.7 jit_solution(1947284333361985190)
XLA Ops:
  0.6 0.5 %collective-permute-start = (bf16[8,2,1280]{2,1,0:T(2,128)(2,1)}, bf16[8,2,1280]{2,1,0:T(2,128)(2,1)S(1)}, u32[]{:S(2)}, u32[]{:S(2)}) collective-permute-start(bf16[8,2,1280]{2,1,0:T(2,128)(2,1)} %images_ref.1), channel_id=1, source_target_pairs={{0,1},{1,0},{2,3},{3,2},{4,5},{5,4},{6,7},{7,6},{8,9},{9,8},{10,11... | collective-permute-start | bytes 122888 | tf_op jit(solution)/shard_map/ppermute | solution.py:25
  1.1 0.8 %copy-done = bf16[8,2,1280]{2,1,0:T(2,128)(2,1)S(1)} copy-done((bf16[8,2,1280]{2,1,0:T(2,128)(2,1)S(1)}, bf16[8,2,1280]{2,1,0:T(2,128)(2,1)}, u32[]{:S(2)}) %copy-start) | copy-done | bytes 40984
  2.7 4.8 %collective-permute-start.3 = (bf16[16,1280]{1,0:T(8,128)(2,1)S(1)}, bf16[16,1280]{1,0:T(8,128)(2,1)S(1)}, u32[]{:S(2)}, u32[]{:S(2)}) collective-permute-start(bf16[16,1280]{1,0:T(8,128)(2,1)S(1)} %shard_map.42), channel_id=1, source_target_pairs={{0,12},{1,13},{2,14},{3,15},{4,8},{5,9},{6,10},{7,11},{8,4},{9,5},... | collective-permute-start | bytes 122888 | tf_op jit(solution)/shard_map/ppermute | solution.py:25
  7.5 0.6 %collective-permute-start.1 = (bf16[16,1280]{1,0:T(8,128)(2,1)S(1)}, bf16[16,1280]{1,0:T(8,128)(2,1)S(1)}, u32[]{:S(2)}, u32[]{:S(2)}) collective-permute-start(bf16[16,1280]{1,0:T(8,128)(2,1)S(1)} %shard_map.42), channel_id=1, source_target_pairs={{0,4},{1,5},{2,6},{3,7},{4,0},{5,1},{6,2},{7,3},{8,12},{9,13},{10,... | collective-permute-start | bytes 122888 | tf_op jit(solution)/shard_map/ppermute | solution.py:25
  8.1 1.7 %pad_maximum_fusion.w_ref = bf16[1280,1024]{1,0:T(8,128)(2,1)S(1)} fusion(bf16[1280,512]{1,0:T(8,128)(2,1)S(1)} %collective-permute-done.4, bf16[1280,512]{1,0:T(8,128)(2,1)} %param.3), kind=kLoop, calls=%fused_computation | loop fusion | flops 5242880 | bytes 5242880 | tf_op jit(solution)/shard_map/concatenate | solution.py:212
  9.8 2.6 %collective-permute-done.2 = bf16[16,1280]{1,0:T(8,128)(2,1)S(1)} collective-permute-done((bf16[16,1280]{1,0:T(8,128)(2,1)S(1)}, bf16[16,1280]{1,0:T(8,128)(2,1)S(1)}, u32[]{:S(2)}, u32[]{:S(2)}) %collective-permute-start.2) | collective-permute-done | bytes 40992 | tf_op jit(solution)/shard_map/ppermute | solution.py:25
  12.4 1.6 %collective-permute-start.5 = (bf16[64,1280]{1,0:T(8,128)(2,1)S(1)}, bf16[64,1280]{1,0:T(8,128)(2,1)S(1)}, u32[]{:S(2)}, u32[]{:S(2)}) collective-permute-start(bf16[64,1280]{1,0:T(8,128)(2,1)S(1)} %pad_maximum_fusion.2), channel_id=1, source_target_pairs={{0,2},{1,3},{2,0},{3,1},{4,6},{5,7},{6,4},{7,5},{8,10},{9,11},{10,... | collective-permute-start | bytes 491528 | tf_op jit(solution)/shard_map/ppermute | solution.py:25
  13.9 0.6 %fusion.7.near_ref = f32[64,1024]{1,0:T(8,128)S(1)} fusion(bf16[64,1280]{1,0:T(8,128)(2,1)S(1)} %pad_maximum_fusion.2, bf16[1280,1024]{1,0:T(8,128)(2,1)S(1)} %pad_maximum_fusion.w_ref), kind=kOutput, calls=%fused_computation.13 | convolution fusion | flops 167772160 | bytes 3047424 | tf_op jit(solution)/shard_map/dot_general | solution.py:204
  14.5 3.4 %collective-permute-done.5 = bf16[64,1280]{1,0:T(8,128)(2,1)S(1)} collective-permute-done((bf16[64,1280]{1,0:T(8,128)(2,1)S(1)}, bf16[64,1280]{1,0:T(8,128)(2,1)S(1)}, u32[]{:S(2)}, u32[]{:S(2)}) %collective-permute-start.5) | collective-permute-done | bytes 163872 | tf_op jit(solution)/shard_map/ppermute | solution.py:25
  17.9 0.6 %fusion.8.far_ref = f32[64,1024]{1,0:T(8,128)S(1)} fusion(bf16[64,1280]{1,0:T(8,128)(2,1)S(1)} %collective-permute-done.5, bf16[1280,1024]{1,0:T(8,128)(2,1)S(1)} %pad_maximum_fusion.w_ref), kind=kOutput, calls=%fused_computation.14 | convolution fusion | flops 167772160 | bytes 3047424 | tf_op jit(solution)/shard_map/dot_general | solution.py:204
  18.9 1.6 %collective-permute-start.8 = (f32[72,128]{1,0:T(8,128)S(1)}, f32[72,128]{1,0:T(8,128)S(1)}, u32[]{:S(2)}, u32[]{:S(2)}) collective-permute-start(f32[72,128]{1,0:T(8,128)S(1)} %get-tuple-element.43), channel_id=1, source_target_pairs={{0,6},{1,7},{2,4},{3,5},{4,2},{5,3},{6,0},{7,1},{8,14},{9,15},{10,... | collective-permute-start | bytes 110600 | tf_op jit(solution)/shard_map/ppermute | solution.py:25
  20.5 1.4 %collective-permute-start.7 = (f32[72,128]{1,0:T(8,128)S(1)}, f32[72,128]{1,0:T(8,128)S(1)}, u32[]{:S(2)}, u32[]{:S(2)}) collective-permute-start(f32[72,128]{1,0:T(8,128)S(1)} %get-tuple-element.43), channel_id=1, source_target_pairs={{0,4},{1,5},{2,6},{3,7},{4,0},{5,1},{6,2},{7,3},{8,12},{9,13},{10,... | collective-permute-start | bytes 110600 | tf_op jit(solution)/shard_map/ppermute | solution.py:25
  21.9 0.5 %collective-permute-start.6 = (f32[72,128]{1,0:T(8,128)S(1)}, f32[72,128]{1,0:T(8,128)S(1)}, u32[]{:S(2)}, u32[]{:S(2)}) collective-permute-start(f32[72,128]{1,0:T(8,128)S(1)} %get-tuple-element.43), channel_id=1, source_target_pairs={{0,2},{1,3},{2,0},{3,1},{4,6},{5,7},{6,4},{7,5},{8,10},{9,11},{10,... | collective-permute-start | bytes 110600 | tf_op jit(solution)/shard_map/ppermute | solution.py:25
  22.5 1.3 %collective-permute-done.8 = f32[72,128]{1,0:T(8,128)S(1)} collective-permute-done((f32[72,128]{1,0:T(8,128)S(1)}, f32[72,128]{1,0:T(8,128)S(1)}, u32[]{:S(2)}, u32[]{:S(2)}) %collective-permute-start.8) | collective-permute-done | bytes 36896 | tf_op jit(solution)/shard_map/ppermute | solution.py:25
  23.8 0.6 %collective-permute-done.7 = f32[72,128]{1,0:T(8,128)S(1)} collective-permute-done((f32[72,128]{1,0:T(8,128)S(1)}, f32[72,128]{1,0:T(8,128)S(1)}, u32[]{:S(2)}, u32[]{:S(2)}) %collective-permute-start.7) | collective-permute-done | bytes 36896 | tf_op jit(solution)/shard_map/ppermute | solution.py:25
  24.4 1.4 %collective-permute-done.6 = f32[72,128]{1,0:T(8,128)S(1)} collective-permute-done((f32[72,128]{1,0:T(8,128)S(1)}, f32[72,128]{1,0:T(8,128)S(1)}, u32[]{:S(2)}, u32[]{:S(2)}) %collective-permute-start.6) | collective-permute-done | bytes 36896 | tf_op jit(solution)/shard_map/ppermute | solution.py:25
  26.0 1.9 %collective-permute-start.9 = (f32[72,128]{1,0:T(8,128)S(1)}, f32[72,128]{1,0:T(8,128)S(1)}, u32[]{:S(2)}, u32[]{:S(2)}) collective-permute-start(f32[72,128]{1,0:T(8,128)S(1)} %add_add_fusion), channel_id=1, source_target_pairs={{0,8},{1,9},{2,10},{3,11},{4,12},{5,13},{6,14},{7,15},{8,0},{9,1},... | collective-permute-start | bytes 110600 | tf_op jit(solution)/shard_map/ppermute | solution.py:25
  28.1 1.6 %collective-permute-start.18 = (bf16[128,1280]{1,0:T(8,128)(2,1)S(1)}, bf16[128,1280]{1,0:T(8,128)(2,1)S(1)}, u32[]{:S(2)}, u32[]{:S(2)}) collective-permute-start(bf16[128,1280]{1,0:T(8,128)(2,1)S(1)} %pad_maximum_fusion.1.refs_0_), channel_id=1, source_target_pairs={{0,16},{16,0},{1,17},{17,1},{2,18},{18,2},{3,19},{19,3},{4,20},{20... | collective-permute-start | bytes 983048 | tf_op jit(solution)/shard_map/ppermute | solution.py:199
  29.7 0.5 %fusion.9.other_ref = f32[128,1024]{1,0:T(8,128)S(1)} fusion(bf16[128,1280]{1,0:T(8,128)(2,1)S(1)} %collective-permute-done.10.refs_1_, bf16[1280,1024]{1,0:T(8,128)(2,1)S(1)} %pad_maximum_fusion.w_ref), kind=kOutput, calls=%fused_computation.15 | convolution fusion | flops 335544320 | bytes 3473408 | tf_op jit(solution)/shard_map/dot_general | solution.py:204
  30.2 1.3 %collective-permute-done.9 = f32[72,128]{1,0:T(8,128)S(1)} collective-permute-done((f32[72,128]{1,0:T(8,128)S(1)}, f32[72,128]{1,0:T(8,128)S(1)}, u32[]{:S(2)}, u32[]{:S(2)}) %collective-permute-start.9) | collective-permute-done | bytes 36896 | tf_op jit(solution)/shard_map/ppermute | solution.py:25
  31.5 1.5 %shard_map.45 = (bf16[128,1024]{1,0:T(8,128)(2,1)S(1)}, bf16[64,1280]{1,0:T(8,128)(2,1)S(1)}) custom-call(s32[1]{0:T(128)} %bitcast.me_ref, f32[72,128]{1,0:T(8,128)S(1)} %add.27.packed_ref, bf16[128,1024]{1,0:T(8,128)(2,1)S(1)} %get-tuple-element.50.c_ref, f32[64,1024]{1,0:T(8,128)S(1)} %fusion.7.near_ref, f32[64,1024]{1,0:T(8,128)S(1)} %fusion.8.far_ref, ...), custom_call_target="tpu_custom_call" | custom-call | tf_op jit(solution)/shard_map/pallas_call | solution.py:246
  33.0 0.6 %collective-permute-start.11 = (bf16[64,1280]{1,0:T(8,128)(2,1)S(1)}, bf16[64,1280]{1,0:T(8,128)(2,1)S(1)}, u32[]{:S(2)}, u32[]{:S(2)}) collective-permute-start(bf16[64,1280]{1,0:T(8,128)(2,1)S(1)} %get-tuple-element.55), channel_id=1, source_target_pairs={{0,2},{1,3},{2,0},{3,1},{4,6},{5,7},{6,4},{7,5},{8,10},{9,11},{10,... | collective-permute-start | bytes 491528 | tf_op jit(solution)/shard_map/ppermute | solution.py:25
  33.6 0.9 %fusion = f32[64,1280]{1,0:T(8,128)S(1)} fusion(bf16[1280,1024]{1,0:T(8,128)(2,1)S(1)} %pad_maximum_fusion.w_ref, bf16[128,1024]{1,0:T(8,128)(2,1)S(1)} %get-tuple-element.57.refs_2_), kind=kOutput, calls=%fused_computation.4 | convolution fusion | flops 167772160 | bytes 3080192 | tf_op jit(solution)/shard_map/dot_general | solution.py:39
  34.5 1.6 %collective-permute-start.15 = (bf16[128,1024]{1,0:T(8,128)(2,1)S(1)}, bf16[128,1024]{1,0:T(8,128)(2,1)S(1)}, u32[]{:S(2)}, u32[]{:S(2)}) collective-permute-start(bf16[128,1024]{1,0:T(8,128)(2,1)S(1)} %get-tuple-element.57.refs_2_), channel_id=1, source_target_pairs={{0,16},{16,0},{1,17},{17,1},{2,18},{18,2},{3,19},{19,3},{4,20},{20... | collective-permute-start | bytes 786440 | tf_op jit(solution)/shard_map/ppermute | solution.py:199
  36.1 3.0 %collective-permute-done.11 = bf16[64,1280]{1,0:T(8,128)(2,1)S(1)} collective-permute-done((bf16[64,1280]{1,0:T(8,128)(2,1)S(1)}, bf16[64,1280]{1,0:T(8,128)(2,1)S(1)}, u32[]{:S(2)}, u32[]{:S(2)}) %collective-permute-start.11) | collective-permute-done | bytes 163872 | tf_op jit(solution)/shard_map/ppermute | solution.py:25
  39.2 1.7 %collective-permute-start.14 = (bf16[16,1280]{1,0:T(8,128)(2,1)S(1)}, bf16[16,1280]{1,0:T(8,128)(2,1)S(1)}, u32[]{:S(2)}, u32[]{:S(2)}) collective-permute-start(bf16[16,1280]{1,0:T(8,128)(2,1)S(1)} %get-tuple-element.68), channel_id=1, source_target_pairs={{0,12},{1,13},{2,14},{3,15},{4,8},{5,9},{6,10},{7,11},{8,4},{9,5},... | collective-permute-start | bytes 122888 | tf_op jit(solution)/shard_map/ppermute | solution.py:25
  40.9 2.8 %collective-permute-start.12 = (bf16[16,1280]{1,0:T(8,128)(2,1)S(1)}, bf16[16,1280]{1,0:T(8,128)(2,1)S(1)}, u32[]{:S(2)}, u32[]{:S(2)}) collective-permute-start(bf16[16,1280]{1,0:T(8,128)(2,1)S(1)} %get-tuple-element.70), channel_id=1, source_target_pairs={{0,4},{1,5},{2,6},{3,7},{4,0},{5,1},{6,2},{7,3},{8,12},{9,13},{10,... | collective-permute-start | bytes 122888 | tf_op jit(solution)/shard_map/ppermute | solution.py:25
  43.7 0.6 %collective-permute-start.20 = (bf16[128,512]{1,0:T(8,128)(2,1)S(1)}, bf16[128,512]{1,0:T(8,128)(2,1)S(1)}, u32[]{:S(2)}, u32[]{:S(2)}) collective-permute-start(bf16[128,512]{1,0:T(8,128)(2,1)S(1)} %slice.42), channel_id=1, source_target_pairs={{0,1},{1,0},{2,3},{3,2},{4,5},{5,4},{6,7},{7,6},{8,9},{9,8},{10,11... | collective-permute-start | bytes 393224 | tf_op jit(solution)/shard_map/ppermute | solution.py:25
  44.3 0.5 %shard_map.46.refs_4_ = f32[1280,512]{1,0:T(8,128)S(1)} custom-call(bf16[128,1280]{1,0:T(8,128)(2,1)S(1)} %pad_maximum_fusion.1.refs_0_, bf16[128,1280]{1,0:T(8,128)(2,1)S(1)} %collective-permute-done.10.refs_1_, bf16[128,1024]{1,0:T(8,128)(2,1)S(1)} %get-tuple-element.57.refs_2_, bf16[128,512]{1,0:T(8,128)(2,1)S(1)} %collective-permute-done.16.refs_3_), custom_call_target="tpu_custom_call" | custom-call | tf_op jit(solution)/shard_map/pallas_call | solution.py:254
  45.1 1.0 %collective-permute-done.13 = bf16[16,1280]{1,0:T(8,128)(2,1)S(1)} collective-permute-done((bf16[16,1280]{1,0:T(8,128)(2,1)S(1)}, bf16[16,1280]{1,0:T(8,128)(2,1)S(1)}, u32[]{:S(2)}, u32[]{:S(2)}) %collective-permute-start.13) | collective-permute-done | bytes 40992 | tf_op jit(solution)/shard_map/ppermute | solution.py:25
  46.2 1.8 %shard_map.47 = f32[1280,512]{1,0:T(8,128)} custom-call(bf16[128,1280]{1,0:T(8,128)(2,1)S(1)} %collective-permute-done.18.refs_0_, bf16[128,1280]{1,0:T(8,128)(2,1)S(1)} %collective-permute-done.19.refs_1_, bf16[128,1024]{1,0:T(8,128)(2,1)S(1)} %collective-permute-done.15.refs_2_, bf16[128,512]{1,0:T(8,128)(2,1)S(1)} %collective-permute-done.20.refs_3_, ...), custom_call_target="tpu_custom_call" | custom-call | tf_op jit(solution)/shard_map/pallas_call | solution.py:281
  48.0 0.7 %shard_map.48 = f32[8,2,1280]{2,1,0:T(2,128)} custom-call(s32[1]{0:T(128)} %bitcast.me_ref, f32[8,1280]{1,0:T(8,128)S(1)} %get-tuple-element.72.own_ref, f32[8,1280]{1,0:T(8,128)S(1)} %collective-permute-done.17.other_ref), custom_call_target="tpu_custom_call" | custom-call | tf_op jit(solution)/shard_map/pallas_call | solution.py:290
  (35 shorter events, 2.0 us)
Async XLA Ops:
  0.6 1.6 %collective-permute-start = (bf16[8,2,1280]{2,1,0:T(2,128)(2,1)}, bf16[8,2,1280]{2,1,0:T(2,128)(2,1)S(1)}, u32[]{:S(2)}, u32[]{:S(2)}) collective-permute-start(bf16[8,2,1280]{2,1,0:T(2,128)(2,1)} %images_ref.1), channel_id=1, source_target_pairs={{0,1},{1,0},{2,3},{3,2},{4,5},{5,4},{6,7},{7,6},{8,9},{9,8},{10,11... | collective-permute-start | bytes 122888 | tf_op jit(solution)/shard_map/ppermute | solution.py:25
  1.1 0.8 %copy-start = (bf16[8,2,1280]{2,1,0:T(2,128)(2,1)S(1)}, bf16[8,2,1280]{2,1,0:T(2,128)(2,1)}, u32[]{:S(2)}) copy-start(bf16[8,2,1280]{2,1,0:T(2,128)(2,1)} %images_ref.1) | copy-start | bytes 122884
  2.2 5.9 %collective-permute-start.4 = (bf16[1280,512]{1,0:T(8,128)(2,1)}, bf16[1280,512]{1,0:T(8,128)(2,1)S(1)}, u32[]{:S(2)}, u32[]{:S(2)}) collective-permute-start(bf16[1280,512]{1,0:T(8,128)(2,1)} %param.3), channel_id=1, source_target_pairs={{0,1},{1,0},{2,3},{3,2},{4,5},{5,4},{6,7},{7,6},{8,9},{9,8},{10,11... | collective-permute-start | bytes 3932168 | tf_op jit(solution)/shard_map/ppermute | solution.py:25
  2.7 7.1 %collective-permute-start.3 = (bf16[16,1280]{1,0:T(8,128)(2,1)S(1)}, bf16[16,1280]{1,0:T(8,128)(2,1)S(1)}, u32[]{:S(2)}, u32[]{:S(2)}) collective-permute-start(bf16[16,1280]{1,0:T(8,128)(2,1)S(1)} %shard_map.42), channel_id=1, source_target_pairs={{0,12},{1,13},{2,14},{3,15},{4,8},{5,9},{6,10},{7,11},{8,4},{9,5},... | collective-permute-start | bytes 122888 | tf_op jit(solution)/shard_map/ppermute | solution.py:25
  7.5 4.9 %collective-permute-start.2 = (bf16[16,1280]{1,0:T(8,128)(2,1)S(1)}, bf16[16,1280]{1,0:T(8,128)(2,1)S(1)}, u32[]{:S(2)}, u32[]{:S(2)}) collective-permute-start(bf16[16,1280]{1,0:T(8,128)(2,1)S(1)} %shard_map.42), channel_id=1, source_target_pairs={{0,8},{1,9},{2,10},{3,11},{4,12},{5,13},{6,14},{7,15},{8,0},{9,1},... | collective-permute-start | bytes 122888 | tf_op jit(solution)/shard_map/ppermute | solution.py:25
  7.5 4.9 %collective-permute-start.1 = (bf16[16,1280]{1,0:T(8,128)(2,1)S(1)}, bf16[16,1280]{1,0:T(8,128)(2,1)S(1)}, u32[]{:S(2)}, u32[]{:S(2)}) collective-permute-start(bf16[16,1280]{1,0:T(8,128)(2,1)S(1)} %shard_map.42), channel_id=1, source_target_pairs={{0,4},{1,5},{2,6},{3,7},{4,0},{5,1},{6,2},{7,3},{8,12},{9,13},{10,... | collective-permute-start | bytes 122888 | tf_op jit(solution)/shard_map/ppermute | solution.py:25
  12.4 5.5 %collective-permute-start.5 = (bf16[64,1280]{1,0:T(8,128)(2,1)S(1)}, bf16[64,1280]{1,0:T(8,128)(2,1)S(1)}, u32[]{:S(2)}, u32[]{:S(2)}) collective-permute-start(bf16[64,1280]{1,0:T(8,128)(2,1)S(1)} %pad_maximum_fusion.2), channel_id=1, source_target_pairs={{0,2},{1,3},{2,0},{3,1},{4,6},{5,7},{6,4},{7,5},{8,10},{9,11},{10,... | collective-permute-start | bytes 491528 | tf_op jit(solution)/shard_map/ppermute | solution.py:25
  18.9 4.9 %collective-permute-start.8 = (f32[72,128]{1,0:T(8,128)S(1)}, f32[72,128]{1,0:T(8,128)S(1)}, u32[]{:S(2)}, u32[]{:S(2)}) collective-permute-start(f32[72,128]{1,0:T(8,128)S(1)} %get-tuple-element.43), channel_id=1, source_target_pairs={{0,6},{1,7},{2,4},{3,5},{4,2},{5,3},{6,0},{7,1},{8,14},{9,15},{10,... | collective-permute-start | bytes 110600 | tf_op jit(solution)/shard_map/ppermute | solution.py:25
  20.5 4.0 %collective-permute-start.7 = (f32[72,128]{1,0:T(8,128)S(1)}, f32[72,128]{1,0:T(8,128)S(1)}, u32[]{:S(2)}, u32[]{:S(2)}) collective-permute-start(f32[72,128]{1,0:T(8,128)S(1)} %get-tuple-element.43), channel_id=1, source_target_pairs={{0,4},{1,5},{2,6},{3,7},{4,0},{5,1},{6,2},{7,3},{8,12},{9,13},{10,... | collective-permute-start | bytes 110600 | tf_op jit(solution)/shard_map/ppermute | solution.py:25
  21.9 4.0 %collective-permute-start.6 = (f32[72,128]{1,0:T(8,128)S(1)}, f32[72,128]{1,0:T(8,128)S(1)}, u32[]{:S(2)}, u32[]{:S(2)}) collective-permute-start(f32[72,128]{1,0:T(8,128)S(1)} %get-tuple-element.43), channel_id=1, source_target_pairs={{0,2},{1,3},{2,0},{3,1},{4,6},{5,7},{6,4},{7,5},{8,10},{9,11},{10,... | collective-permute-start | bytes 110600 | tf_op jit(solution)/shard_map/ppermute | solution.py:25
  25.9 3.9 %collective-permute-start.10 = (bf16[128,1280]{1,0:T(8,128)(2,1)S(1)}, bf16[128,1280]{1,0:T(8,128)(2,1)S(1)}, u32[]{:S(2)}, u32[]{:S(2)}) collective-permute-start(bf16[128,1280]{1,0:T(8,128)(2,1)S(1)} %pad_maximum_fusion.1.refs_0_), channel_id=1, source_target_pairs={{0,1},{1,0},{2,3},{3,2},{4,5},{5,4},{6,7},{7,6},{8,9},{9,8},{10,11... | collective-permute-start | bytes 983048 | tf_op jit(solution)/shard_map/ppermute | solution.py:25
  26.0 5.6 %collective-permute-start.9 = (f32[72,128]{1,0:T(8,128)S(1)}, f32[72,128]{1,0:T(8,128)S(1)}, u32[]{:S(2)}, u32[]{:S(2)}) collective-permute-start(f32[72,128]{1,0:T(8,128)S(1)} %add_add_fusion), channel_id=1, source_target_pairs={{0,8},{1,9},{2,10},{3,11},{4,12},{5,13},{6,14},{7,15},{8,0},{9,1},... | collective-permute-start | bytes 110600 | tf_op jit(solution)/shard_map/ppermute | solution.py:25
  28.1 12.7 %collective-permute-start.18 = (bf16[128,1280]{1,0:T(8,128)(2,1)S(1)}, bf16[128,1280]{1,0:T(8,128)(2,1)S(1)}, u32[]{:S(2)}, u32[]{:S(2)}) collective-permute-start(bf16[128,1280]{1,0:T(8,128)(2,1)S(1)} %pad_maximum_fusion.1.refs_0_), channel_id=1, source_target_pairs={{0,16},{16,0},{1,17},{17,1},{2,18},{18,2},{3,19},{19,3},{4,20},{20... | collective-permute-start | bytes 983048 | tf_op jit(solution)/shard_map/ppermute | solution.py:199
  33.0 6.1 %collective-permute-start.11 = (bf16[64,1280]{1,0:T(8,128)(2,1)S(1)}, bf16[64,1280]{1,0:T(8,128)(2,1)S(1)}, u32[]{:S(2)}, u32[]{:S(2)}) collective-permute-start(bf16[64,1280]{1,0:T(8,128)(2,1)S(1)} %get-tuple-element.55), channel_id=1, source_target_pairs={{0,2},{1,3},{2,0},{3,1},{4,6},{5,7},{6,4},{7,5},{8,10},{9,11},{10,... | collective-permute-start | bytes 491528 | tf_op jit(solution)/shard_map/ppermute | solution.py:25
  34.5 9.1 %collective-permute-start.15 = (bf16[128,1024]{1,0:T(8,128)(2,1)S(1)}, bf16[128,1024]{1,0:T(8,128)(2,1)S(1)}, u32[]{:S(2)}, u32[]{:S(2)}) collective-permute-start(bf16[128,1024]{1,0:T(8,128)(2,1)S(1)} %get-tuple-element.57.refs_2_), channel_id=1, source_target_pairs={{0,16},{16,0},{1,17},{17,1},{2,18},{18,2},{3,19},{19,3},{4,20},{20... | collective-permute-start | bytes 786440 | tf_op jit(solution)/shard_map/ppermute | solution.py:199
  36.1 7.6 %collective-permute-start.16 = (bf16[128,512]{1,0:T(8,128)(2,1)S(1)}, bf16[128,512]{1,0:T(8,128)(2,1)S(1)}, u32[]{:S(2)}, u32[]{:S(2)}) collective-permute-start(bf16[128,512]{1,0:T(8,128)(2,1)S(1)} %slice.39), channel_id=1, source_target_pairs={{0,1},{1,0},{2,3},{3,2},{4,5},{5,4},{6,7},{7,6},{8,9},{9,8},{10,11... | collective-permute-start | bytes 393224 | tf_op jit(solution)/shard_map/ppermute | solution.py:25
  39.2 5.9 %collective-permute-start.14 = (bf16[16,1280]{1,0:T(8,128)(2,1)S(1)}, bf16[16,1280]{1,0:T(8,128)(2,1)S(1)}, u32[]{:S(2)}, u32[]{:S(2)}) collective-permute-start(bf16[16,1280]{1,0:T(8,128)(2,1)S(1)} %get-tuple-element.68), channel_id=1, source_target_pairs={{0,12},{1,13},{2,14},{3,15},{4,8},{5,9},{6,10},{7,11},{8,4},{9,5},... | collective-permute-start | bytes 122888 | tf_op jit(solution)/shard_map/ppermute | solution.py:25
  40.8 5.2 %collective-permute-start.13 = (bf16[16,1280]{1,0:T(8,128)(2,1)S(1)}, bf16[16,1280]{1,0:T(8,128)(2,1)S(1)}, u32[]{:S(2)}, u32[]{:S(2)}) collective-permute-start(bf16[16,1280]{1,0:T(8,128)(2,1)S(1)} %get-tuple-element.69), channel_id=1, source_target_pairs={{0,8},{1,9},{2,10},{3,11},{4,12},{5,13},{6,14},{7,15},{8,0},{9,1},... | collective-permute-start | bytes 122888 | tf_op jit(solution)/shard_map/ppermute | solution.py:25
  40.9 5.2 %collective-permute-start.12 = (bf16[16,1280]{1,0:T(8,128)(2,1)S(1)}, bf16[16,1280]{1,0:T(8,128)(2,1)S(1)}, u32[]{:S(2)}, u32[]{:S(2)}) collective-permute-start(bf16[16,1280]{1,0:T(8,128)(2,1)S(1)} %get-tuple-element.70), channel_id=1, source_target_pairs={{0,4},{1,5},{2,6},{3,7},{4,0},{5,1},{6,2},{7,3},{8,12},{9,13},{10,... | collective-permute-start | bytes 122888 | tf_op jit(solution)/shard_map/ppermute | solution.py:25
  43.7 2.5 %collective-permute-start.19 = (bf16[128,1280]{1,0:T(8,128)(2,1)S(1)}, bf16[128,1280]{1,0:T(8,128)(2,1)S(1)}, u32[]{:S(2)}, u32[]{:S(2)}) collective-permute-start(bf16[128,1280]{1,0:T(8,128)(2,1)S(1)} %collective-permute-done.18.refs_0_), channel_id=1, source_target_pairs={{0,1},{1,0},{2,3},{3,2},{4,5},{5,4},{6,7},{7,6},{8,9},{9,8},{10,11... | collective-permute-start | bytes 983048 | tf_op jit(solution)/shard_map/ppermute | solution.py:25
  43.7 2.5 %collective-permute-start.20 = (bf16[128,512]{1,0:T(8,128)(2,1)S(1)}, bf16[128,512]{1,0:T(8,128)(2,1)S(1)}, u32[]{:S(2)}, u32[]{:S(2)}) collective-permute-start(bf16[128,512]{1,0:T(8,128)(2,1)S(1)} %slice.42), channel_id=1, source_target_pairs={{0,1},{1,0},{2,3},{3,2},{4,5},{5,4},{6,7},{7,6},{8,9},{9,8},{10,11... | collective-permute-start | bytes 393224 | tf_op jit(solution)/shard_map/ppermute | solution.py:25
  46.1 1.9 %collective-permute-start.17 = (f32[8,1280]{1,0:T(8,128)S(1)}, f32[8,1280]{1,0:T(8,128)S(1)}, u32[]{:S(2)}, u32[]{:S(2)}) collective-permute-start(f32[8,1280]{1,0:T(8,128)S(1)} %get-tuple-element.71), channel_id=1, source_target_pairs={{0,1},{1,0},{2,3},{3,2},{4,5},{5,4},{6,7},{7,6},{8,9},{9,8},{10,11... | collective-permute-start | bytes 122888 | tf_op jit(solution)/shard_map/ppermute | solution.py:25
